TPU v7x, 32 devices: a whole 2x2x4 slice. The times are simulated.
32 devices in a mesh: box: 8 (over y, x, core), copy: 4 (over z).
Axes of the slice: x: 2, y: 2, z: 4, core: 2. Of those that a mesh axis runs over, the one named last changes fastest.
Arguments:
- positions: float32 [2048, 3, 128], P(('copy', 'box')), parts along dimension 0, may hold values from 0 to 1
- charges: float32 [2048, 128], P(('copy', 'box')), parts along dimension 0, may hold values from -0.1875 to 0.1875
- counts: int32 [2048], P(('copy', 'box')), parts along dimension 0, may hold values from 1 to 128
- multipoles: float32 [2048, 121], P(('copy', 'box')), parts along dimension 0, may hold values from -6 to 6
- device_local: float32 [32, 121], P(('copy', 'box')), parts along dimension 0, may hold values from -6 to 6
- m2l_sources: int32 [2048, 16], P(('copy', 'box')), parts along dimension 0, may hold values from 0 to 511, as said below
- m2l_kinds: int32 [2048, 16], P(('copy', 'box')), parts along dimension 0, may hold values from 0 to 31, as said below
- m2l_ops: float32 [32, 121, 121], replicated, may hold values from -0.125 to 0.125
- l2l_ops: float32 [8, 121, 121], replicated, may hold values from -0.5 to 0.5
Outputs:
- near_potential: float32 [2048, 128], P(('copy', 'box')), parts along dimension 0
- leaf_local: float32 [2048, 121], P(('copy', 'box')), parts along dimension 0
There are 4 independent parts, one for each index of `copy`. A program takes and returns all parts, laid end to end along the dimension named above; an argument that names none is the same for every part. Nothing has to cross between parts.
Inputs may be any that keep to these rules, and one draw needn't show every extreme that they name: `counts`: slots from the count on are padding. `m2l_sources`: the entries of a leaf are distinct children of boxes adjacent (periodically) to the leaf's parent, none adjacent to the leaf itself. `m2l_kinds`: entries with the same offset from source to target leaf have the same kind.
All inputs are finite; a program needn't handle non-finite values.
Results may differ from a plain program's by a relative error of at most 0.0003.
Values sent between devices are 32-bit elements; how exact they have to be, the bound alone decides.
A program may use at most 64 MiB of HBM per device.

v0:
```python
import jax
import jax.numpy as jnp
from jax import lax
from jax.sharding import PartitionSpec as P

SOFTENING_SQ = 0.0025


def from_partner(value, axis, stride):
    mask = 2**stride
    pairs = [(source, source ^ mask) for source in range(lax.axis_size(axis))]
    return lax.ppermute(value, axis, pairs)


def split_code(code_value, bit_count):
    coords_out = []
    for axis_id in range(3):
        result = jnp.zeros_like(code_value)
        for bit_id in range(bit_count):
            result = result + code_value // 2 ** (3 * bit_id + axis_id) % 2 * 2**bit_id
        coords_out.append(result)
    return coords_out


def join_code(coords_in, bit_count):
    result = jnp.zeros_like(coords_in[0])
    for axis_id in range(3):
        for bit_id in range(bit_count):
            result = result + coords_in[axis_id] // 2**bit_id % 2 * 2 ** (3 * bit_id + axis_id)
    return result


def offset_table():
    rows_list = [
        [offset_id // 9 - 1, offset_id // 3 % 3 - 1, offset_id % 3 - 1] for offset_id in range(27)
    ]
    return jnp.array(rows_list, dtype=jnp.float32)


def self_mask(tile_slots):
    slot_ids = jnp.arange(tile_slots)
    same_slot = slot_ids[:, None] == slot_ids[None, :]
    center = jnp.arange(27) == 13
    return center[:, None, None] & same_slot[None, :, :]


def block_potential(targets, sources, source_charge, offsets, excluded):
    dist_sq = jnp.zeros((targets.shape[0], 27, targets.shape[2], sources.shape[3]), jnp.float32)
    for axis_id in range(3):
        gap = (
            offsets[None, :, axis_id, None, None]
            + sources[:, :, axis_id, None, :]
            - targets[:, None, axis_id, :, None]
        )
        dist_sq = dist_sq + gap * gap
    inverse = jnp.where(excluded[None], 0.0, lax.rsqrt(dist_sq + SOFTENING_SQ))
    return jnp.einsum("bopq,boq->bp", inverse, source_charge, precision=lax.Precision.HIGHEST)


def swap_faces(payload, bit_id):
    return from_partner(payload, "box", bit_id)


def local(
    positions, charges, counts, multipoles, device_local, m2l_sources, m2l_kinds, m2l_ops, l2l_ops
):
    box_count = lax.axis_size("box")
    own_box = lax.axis_index("box")
    per_box = positions.shape[0]
    tile_slots = positions.shape[2]
    terms_count = multipoles.shape[1]
    leaf_side = 2
    while leaf_side**3 < per_box:
        leaf_side = leaf_side * 2
    grid_count = 2
    while grid_count**3 < box_count:
        grid_count = grid_count * 2
    grid_bits = grid_count.bit_length() - 1
    side_bits = leaf_side.bit_length() - 1
    live_mask = jnp.arange(tile_slots)[None, :] < counts[:, None]
    charge_live = jnp.where(live_mask, charges, 0.0)
    tiles = jnp.concatenate([positions, charge_live[:, None, :]], axis=1)
    cell_ids = jnp.arange(per_box, dtype=jnp.int32)
    cell_code = join_code(
        [
            cell_ids // (leaf_side * leaf_side),
            cell_ids // leaf_side % leaf_side,
            cell_ids % leaf_side,
        ],
        side_bits,
    )
    grid = tiles[cell_code].reshape(leaf_side, leaf_side, leaf_side, 4, tile_slots)
    block_place = split_code(own_box, grid_bits)
    for axis_id in range(3):
        width_now = grid.shape[axis_id]
        lower_face = lax.slice_in_dim(grid, 0, 1, 1, axis_id)
        upper_face = lax.slice_in_dim(grid, width_now - 1, width_now, 1, axis_id)
        even = block_place[axis_id] % 2 == 0
        toward = jnp.where(even, upper_face, lower_face)
        away = jnp.where(even, lower_face, upper_face)
        received = swap_faces(jnp.stack([toward, away]), axis_id)
        first_face = received[0]
        second_face = received[1]
        if grid_bits == 2:
            second_face = swap_faces(second_face, 3 + axis_id)
        below = jnp.where(even, second_face, first_face)
        above = jnp.where(even, first_face, second_face)
        grid = jnp.concatenate([below, grid, above], axis=axis_id)
    padded_side = leaf_side + 2
    pool = grid.reshape(padded_side**3, 4, tile_slots)
    inner_place = split_code(cell_ids, side_bits)
    columns = []
    for offset_id in range(27):
        deltas = (offset_id // 9 - 1, offset_id // 3 % 3 - 1, offset_id % 3 - 1)
        spots = [inner_place[axis_id] + 1 + deltas[axis_id] for axis_id in range(3)]
        columns.append((spots[0] * padded_side + spots[1]) * padded_side + spots[2])
    place = jnp.stack(columns, axis=-1)
    gathered_tiles = pool[place]
    source_pos = gathered_tiles[:, :, 0:3, :]
    source_charge = gathered_tiles[:, :, 3, :]
    offsets = offset_table()
    excluded = self_mask(tile_slots)
    block_count = per_box // 4

    def near_block(items):
        return block_potential(items[0], items[1], items[2], offsets, excluded)

    near = lax.map(
        near_block,
        (
            positions.reshape(block_count, 4, 3, tile_slots),
            source_pos.reshape(block_count, 4, 27, 3, tile_slots),
            source_charge.reshape(block_count, 4, 27, tile_slots),
        ),
    )
    near_potential = jnp.where(live_mask, near.reshape(per_box, tile_slots), 0.0)
    all_multipoles = lax.all_gather(multipoles, "box", axis=0, tiled=True)
    gathered = all_multipoles[m2l_sources]

    def translate_leaf(items):
        return jnp.einsum("est,et->s", m2l_ops[items[0]], items[1], precision=lax.Precision.HIGHEST)

    far_terms = lax.map(translate_leaf, (m2l_kinds, gathered))
    descended = device_local
    for step_id in range(leaf_side.bit_length() - 1):
        descended = jnp.einsum(
            "cst,nt->ncs", l2l_ops, descended, precision=lax.Precision.HIGHEST
        ).reshape(-1, terms_count)
    leaf_local = descended + far_terms
    return (near_potential, leaf_local)


def solution(mesh):
    placed = (
        P(("copy", "box"), None, None),
        P(("copy", "box"), None),
        P(("copy", "box")),
        P(("copy", "box"), None),
        P(("copy", "box"), None),
        P(("copy", "box"), None),
        P(("copy", "box"), None),
        P(),
        P(),
    )
    return jax.shard_map(
        local,
        mesh=mesh,
        in_specs=placed,
        out_specs=(P(("copy", "box"), None), P(("copy", "box"), None)),
        check_vma=False,
    )
```

profile of v0, /device:TPU:0, one launch (start us, length us, event | category | flops | bytes accessed | tf_op | source)
XLA Modules:
  0.0 422.0 jit_solution(11264260777784260057)
XLA Ops:
  4.7 4.0 copy.69
  8.7 10.3 %all_gather.3 = f32[512,121]{1,0:T(8,128)S(1)} all-gather(f32[64,121]{1,0:T(8,128)S(1)} %copy-done.1), channel_id=1, replica_groups=mesh['box'=8,'copy'=4] {'box'}, dimensions={0}, use_global_device_ids=true | all-gather | bytes 278784 | tf_op jit(solution)/shard_map/all_gather | solution.py:137
  19.3 2.8 gather_fusion.3
  22.1 206.5 %while.22 = (s32[]{:T(128)}, f32[64,121]{1,0:T(8,128)S(1)}, s32[64,16]{1,0:T(8,128)S(1)}, f32[32,121,121]{2,1,0:T(8,128)}, f32[64,16,121]{2,1,0:T(8,128)S(1)}, /*index=5*/s32[]{:T(128)}, s32[]{:T(128)}) while((s32[]{:T(128)}, f32[64,121]{1,0:T(8,128)S(1)}, s32[64,16]{1,0:T(8,128)S(1)}, f32[32,121,121]{2,1,0:T(8,128)}, ...), condition=%wide.region_3.4_spmd, body=%wide.region_2.3_spmd.sunk | while | flops 2812146 | bytes 2840197 | solution.py:143
  22.2 2.2 gather_fusion
  25.4 2.2 gather_fusion
  28.6 2.2 gather_fusion
  31.9 2.2 gather_fusion
  35.1 2.2 gather_fusion
  38.3 2.2 gather_fusion
  44.8 2.2 gather_fusion
  48.0 2.2 gather_fusion
  51.2 2.2 gather_fusion
  54.5 2.2 gather_fusion
  57.7 2.2 gather_fusion
  60.9 2.2 gather_fusion
  64.1 2.2 gather_fusion
  67.4 2.2 gather_fusion
  77.0 2.2 gather_fusion
  80.3 2.2 gather_fusion
  83.5 2.2 gather_fusion
  86.7 2.2 gather_fusion
  90.0 2.2 gather_fusion
  93.2 2.2 gather_fusion
  96.4 2.2 gather_fusion
  99.6 2.2 gather_fusion
  232.5 3.6 collective-permute-done.1
  237.8 3.8 collective-permute-done.2
  241.8 6.2 %gather_fusion.2 = f32[1728,4,128]{2,1,0:T(4,128)} fusion(f32[216,4,128]{2,1,0:T(4,128)S(1)} %bitcast.183, s32[2048]{0:T(1024)S(1)} %pad_clamp_fusion.1), kind=kCustom, calls=%fused_computation.2 | custom fusion | bytes 7084800 | tf_op jit(solution)/shard_map/gather | solution.py:118
  248.0 2.9 slice.134
  251.0 2.7 copy.63
  254.7 166.6 %while.23 = (s32[]{:T(128)}, f32[16,4,128]{2,1,0:T(4,128)S(1)}, f32[16,4,27,3,128]{4,1,2,3,0:T(4,128)S(1)}, f32[16,4,3,128]{3,2,1,0:T(4,128)S(1)}, f32[16,4,27,1...) while((s32[]{:T(128)}, f32[16,4,128]{2,1,0:T(4,128)S(1)}, ...), condition=%wide.region_1.2_spmd.clone.clone, body=%wide.region_0.1_spmd.sunk.clone.clone.sunk | while | flops 39412224 | bytes 2376156 | solution.py:128
  256.3 9.0 %fusion.85 = f32[4,1,128,1]{2,1,3,0:T(1,128)S(1)} fusion(f32[4,128]{1,0:T(4,128)S(1)} %bitcast.199, f32[4,27,128]{2,1,0:T(8,128)S(1)} %copy.106, f32[4,128]{1,0:T(4,128)S(1)} %bitcast.200, f32[4,27,128]{2,1,0:T(8,128)S(1)} %copy.107, f32[4,128]{1,0:T(4,128)S(1)} %bitcast.198, f32[4,27,128]{2,1,0:T(8,128)S(1)} %copy.108, ...), kind=kOutput, calls=%fused_computation.10.clone.1 | convolution fusion | flops 38928384 | bytes 671744 | tf_op jit(solution)/shard_map/while/body/eval_jaxpr/bopq,boq->bp/dot_general | solution.py:57
  266.7 9.0 %fusion.85 = f32[4,1,128,1]{2,1,3,0:T(1,128)S(1)} fusion(f32[4,128]{1,0:T(4,128)S(1)} %bitcast.199, f32[4,27,128]{2,1,0:T(8,128)S(1)} %copy.106, f32[4,128]{1,0:T(4,128)S(1)} %bitcast.200, f32[4,27,128]{2,1,0:T(8,128)S(1)} %copy.107, f32[4,128]{1,0:T(4,128)S(1)} %bitcast.198, f32[4,27,128]{2,1,0:T(8,128)S(1)} %copy.108, ...), kind=kOutput, calls=%fused_computation.10.clone.1 | convolution fusion | flops 38928384 | bytes 671744 | tf_op jit(solution)/shard_map/while/body/eval_jaxpr/bopq,boq->bp/dot_general | solution.py:57
  277.1 9.0 %fusion.85 = f32[4,1,128,1]{2,1,3,0:T(1,128)S(1)} fusion(f32[4,128]{1,0:T(4,128)S(1)} %bitcast.199, f32[4,27,128]{2,1,0:T(8,128)S(1)} %copy.106, f32[4,128]{1,0:T(4,128)S(1)} %bitcast.200, f32[4,27,128]{2,1,0:T(8,128)S(1)} %copy.107, f32[4,128]{1,0:T(4,128)S(1)} %bitcast.198, f32[4,27,128]{2,1,0:T(8,128)S(1)} %copy.108, ...), kind=kOutput, calls=%fused_computation.10.clone.1 | convolution fusion | flops 38928384 | bytes 671744 | tf_op jit(solution)/shard_map/while/body/eval_jaxpr/bopq,boq->bp/dot_general | solution.py:57
  287.5 9.0 %fusion.85 = f32[4,1,128,1]{2,1,3,0:T(1,128)S(1)} fusion(f32[4,128]{1,0:T(4,128)S(1)} %bitcast.199, f32[4,27,128]{2,1,0:T(8,128)S(1)} %copy.106, f32[4,128]{1,0:T(4,128)S(1)} %bitcast.200, f32[4,27,128]{2,1,0:T(8,128)S(1)} %copy.107, f32[4,128]{1,0:T(4,128)S(1)} %bitcast.198, f32[4,27,128]{2,1,0:T(8,128)S(1)} %copy.108, ...), kind=kOutput, calls=%fused_computation.10.clone.1 | convolution fusion | flops 38928384 | bytes 671744 | tf_op jit(solution)/shard_map/while/body/eval_jaxpr/bopq,boq->bp/dot_general | solution.py:57
  297.9 9.0 %fusion.85 = f32[4,1,128,1]{2,1,3,0:T(1,128)S(1)} fusion(f32[4,128]{1,0:T(4,128)S(1)} %bitcast.199, f32[4,27,128]{2,1,0:T(8,128)S(1)} %copy.106, f32[4,128]{1,0:T(4,128)S(1)} %bitcast.200, f32[4,27,128]{2,1,0:T(8,128)S(1)} %copy.107, f32[4,128]{1,0:T(4,128)S(1)} %bitcast.198, f32[4,27,128]{2,1,0:T(8,128)S(1)} %copy.108, ...), kind=kOutput, calls=%fused_computation.10.clone.1 | convolution fusion | flops 38928384 | bytes 671744 | tf_op jit(solution)/shard_map/while/body/eval_jaxpr/bopq,boq->bp/dot_general | solution.py:57
  308.3 9.0 %fusion.85 = f32[4,1,128,1]{2,1,3,0:T(1,128)S(1)} fusion(f32[4,128]{1,0:T(4,128)S(1)} %bitcast.199, f32[4,27,128]{2,1,0:T(8,128)S(1)} %copy.106, f32[4,128]{1,0:T(4,128)S(1)} %bitcast.200, f32[4,27,128]{2,1,0:T(8,128)S(1)} %copy.107, f32[4,128]{1,0:T(4,128)S(1)} %bitcast.198, f32[4,27,128]{2,1,0:T(8,128)S(1)} %copy.108, ...), kind=kOutput, calls=%fused_computation.10.clone.1 | convolution fusion | flops 38928384 | bytes 671744 | tf_op jit(solution)/shard_map/while/body/eval_jaxpr/bopq,boq->bp/dot_general | solution.py:57
  318.7 9.0 %fusion.85 = f32[4,1,128,1]{2,1,3,0:T(1,128)S(1)} fusion(f32[4,128]{1,0:T(4,128)S(1)} %bitcast.199, f32[4,27,128]{2,1,0:T(8,128)S(1)} %copy.106, f32[4,128]{1,0:T(4,128)S(1)} %bitcast.200, f32[4,27,128]{2,1,0:T(8,128)S(1)} %copy.107, f32[4,128]{1,0:T(4,128)S(1)} %bitcast.198, f32[4,27,128]{2,1,0:T(8,128)S(1)} %copy.108, ...), kind=kOutput, calls=%fused_computation.10.clone.1 | convolution fusion | flops 38928384 | bytes 671744 | tf_op jit(solution)/shard_map/while/body/eval_jaxpr/bopq,boq->bp/dot_general | solution.py:57
  329.1 9.0 %fusion.85 = f32[4,1,128,1]{2,1,3,0:T(1,128)S(1)} fusion(f32[4,128]{1,0:T(4,128)S(1)} %bitcast.199, f32[4,27,128]{2,1,0:T(8,128)S(1)} %copy.106, f32[4,128]{1,0:T(4,128)S(1)} %bitcast.200, f32[4,27,128]{2,1,0:T(8,128)S(1)} %copy.107, f32[4,128]{1,0:T(4,128)S(1)} %bitcast.198, f32[4,27,128]{2,1,0:T(8,128)S(1)} %copy.108, ...), kind=kOutput, calls=%fused_computation.10.clone.1 | convolution fusion | flops 38928384 | bytes 671744 | tf_op jit(solution)/shard_map/while/body/eval_jaxpr/bopq,boq->bp/dot_general | solution.py:57
  339.5 9.0 %fusion.85 = f32[4,1,128,1]{2,1,3,0:T(1,128)S(1)} fusion(f32[4,128]{1,0:T(4,128)S(1)} %bitcast.199, f32[4,27,128]{2,1,0:T(8,128)S(1)} %copy.106, f32[4,128]{1,0:T(4,128)S(1)} %bitcast.200, f32[4,27,128]{2,1,0:T(8,128)S(1)} %copy.107, f32[4,128]{1,0:T(4,128)S(1)} %bitcast.198, f32[4,27,128]{2,1,0:T(8,128)S(1)} %copy.108, ...), kind=kOutput, calls=%fused_computation.10.clone.1 | convolution fusion | flops 38928384 | bytes 671744 | tf_op jit(solution)/shard_map/while/body/eval_jaxpr/bopq,boq->bp/dot_general | solution.py:57
  349.9 9.0 %fusion.85 = f32[4,1,128,1]{2,1,3,0:T(1,128)S(1)} fusion(f32[4,128]{1,0:T(4,128)S(1)} %bitcast.199, f32[4,27,128]{2,1,0:T(8,128)S(1)} %copy.106, f32[4,128]{1,0:T(4,128)S(1)} %bitcast.200, f32[4,27,128]{2,1,0:T(8,128)S(1)} %copy.107, f32[4,128]{1,0:T(4,128)S(1)} %bitcast.198, f32[4,27,128]{2,1,0:T(8,128)S(1)} %copy.108, ...), kind=kOutput, calls=%fused_computation.10.clone.1 | convolution fusion | flops 38928384 | bytes 671744 | tf_op jit(solution)/shard_map/while/body/eval_jaxpr/bopq,boq->bp/dot_general | solution.py:57
  360.3 9.0 %fusion.85 = f32[4,1,128,1]{2,1,3,0:T(1,128)S(1)} fusion(f32[4,128]{1,0:T(4,128)S(1)} %bitcast.199, f32[4,27,128]{2,1,0:T(8,128)S(1)} %copy.106, f32[4,128]{1,0:T(4,128)S(1)} %bitcast.200, f32[4,27,128]{2,1,0:T(8,128)S(1)} %copy.107, f32[4,128]{1,0:T(4,128)S(1)} %bitcast.198, f32[4,27,128]{2,1,0:T(8,128)S(1)} %copy.108, ...), kind=kOutput, calls=%fused_computation.10.clone.1 | convolution fusion | flops 38928384 | bytes 671744 | tf_op jit(solution)/shard_map/while/body/eval_jaxpr/bopq,boq->bp/dot_general | solution.py:57
  370.7 9.0 %fusion.85 = f32[4,1,128,1]{2,1,3,0:T(1,128)S(1)} fusion(f32[4,128]{1,0:T(4,128)S(1)} %bitcast.199, f32[4,27,128]{2,1,0:T(8,128)S(1)} %copy.106, f32[4,128]{1,0:T(4,128)S(1)} %bitcast.200, f32[4,27,128]{2,1,0:T(8,128)S(1)} %copy.107, f32[4,128]{1,0:T(4,128)S(1)} %bitcast.198, f32[4,27,128]{2,1,0:T(8,128)S(1)} %copy.108, ...), kind=kOutput, calls=%fused_computation.10.clone.1 | convolution fusion | flops 38928384 | bytes 671744 | tf_op jit(solution)/shard_map/while/body/eval_jaxpr/bopq,boq->bp/dot_general | solution.py:57
  381.1 9.0 %fusion.85 = f32[4,1,128,1]{2,1,3,0:T(1,128)S(1)} fusion(f32[4,128]{1,0:T(4,128)S(1)} %bitcast.199, f32[4,27,128]{2,1,0:T(8,128)S(1)} %copy.106, f32[4,128]{1,0:T(4,128)S(1)} %bitcast.200, f32[4,27,128]{2,1,0:T(8,128)S(1)} %copy.107, f32[4,128]{1,0:T(4,128)S(1)} %bitcast.198, f32[4,27,128]{2,1,0:T(8,128)S(1)} %copy.108, ...), kind=kOutput, calls=%fused_computation.10.clone.1 | convolution fusion | flops 38928384 | bytes 671744 | tf_op jit(solution)/shard_map/while/body/eval_jaxpr/bopq,boq->bp/dot_general | solution.py:57
  391.5 9.0 %fusion.85 = f32[4,1,128,1]{2,1,3,0:T(1,128)S(1)} fusion(f32[4,128]{1,0:T(4,128)S(1)} %bitcast.199, f32[4,27,128]{2,1,0:T(8,128)S(1)} %copy.106, f32[4,128]{1,0:T(4,128)S(1)} %bitcast.200, f32[4,27,128]{2,1,0:T(8,128)S(1)} %copy.107, f32[4,128]{1,0:T(4,128)S(1)} %bitcast.198, f32[4,27,128]{2,1,0:T(8,128)S(1)} %copy.108, ...), kind=kOutput, calls=%fused_computation.10.clone.1 | convolution fusion | flops 38928384 | bytes 671744 | tf_op jit(solution)/shard_map/while/body/eval_jaxpr/bopq,boq->bp/dot_general | solution.py:57
  401.9 9.0 %fusion.85 = f32[4,1,128,1]{2,1,3,0:T(1,128)S(1)} fusion(f32[4,128]{1,0:T(4,128)S(1)} %bitcast.199, f32[4,27,128]{2,1,0:T(8,128)S(1)} %copy.106, f32[4,128]{1,0:T(4,128)S(1)} %bitcast.200, f32[4,27,128]{2,1,0:T(8,128)S(1)} %copy.107, f32[4,128]{1,0:T(4,128)S(1)} %bitcast.198, f32[4,27,128]{2,1,0:T(8,128)S(1)} %copy.108, ...), kind=kOutput, calls=%fused_computation.10.clone.1 | convolution fusion | flops 38928384 | bytes 671744 | tf_op jit(solution)/shard_map/while/body/eval_jaxpr/bopq,boq->bp/dot_general | solution.py:57
  412.3 9.0 %fusion.85 = f32[4,1,128,1]{2,1,3,0:T(1,128)S(1)} fusion(f32[4,128]{1,0:T(4,128)S(1)} %bitcast.199, f32[4,27,128]{2,1,0:T(8,128)S(1)} %copy.106, f32[4,128]{1,0:T(4,128)S(1)} %bitcast.200, f32[4,27,128]{2,1,0:T(8,128)S(1)} %copy.107, f32[4,128]{1,0:T(4,128)S(1)} %bitcast.198, f32[4,27,128]{2,1,0:T(8,128)S(1)} %copy.108, ...), kind=kOutput, calls=%fused_computation.10.clone.1 | convolution fusion | flops 38928384 | bytes 671744 | tf_op jit(solution)/shard_map/while/body/eval_jaxpr/bopq,boq->bp/dot_general | solution.py:57
  (623 shorter events, 187.5 us)
Async XLA Ops:
  0.6 228.0 %copy-start = (f32[8,121,121]{2,0,1:T(8,128)S(1)}, f32[8,121,121]{2,0,1:T(8,128)}, u32[]{:S(2)}) copy-start(f32[8,121,121]{2,0,1:T(8,128)} %param.22) | copy-start | bytes 1405540
  0.6 8.1 %copy-start.1 = (f32[64,121]{1,0:T(8,128)S(1)}, f32[64,121]{1,0:T(8,128)}, u32[]{:S(2)}) copy-start(f32[64,121]{1,0:T(8,128)} %param.17) | copy-start | bytes 92932
  0.7 18.4 %copy-start.6 = (s32[64,16]{0,1:T(8,128)S(1)}, s32[64,16]{0,1:T(8,128)}, u32[]{:S(2)}) copy-start(s32[64,16]{0,1:T(8,128)} %param.19) | copy-start | bytes 12292
  0.7 18.6 %copy-start.5 = (s32[64,16]{0,1:T(8,128)S(1)}, s32[64,16]{0,1:T(8,128)}, u32[]{:S(2)}) copy-start(s32[64,16]{0,1:T(8,128)} %param.20) | copy-start | bytes 12292
  3.3 227.5 %collective-permute-start = (f32[2,1,4,4,4,128]{5,4,3,2,1,0:T(4,128)S(1)}, f32[2,1,4,4,4,128]{5,4,3,2,1,0:T(4,128)S(1)}, u32[]{:S(2)}, u32[]{:S(2)}) collective-permute-start(f32[2,1,4,4,4,128]{5,4,3,2,1,0:T(4,128)S(1)} %pad_maximum_fusion.8), channel_id=1, source_target_pairs={{0,4},{4,0},{8,12},{12,8},{16,20},{20,16},{24,28},{28,24},{1,5},{5... | collective-permute-start | bytes 196616 | tf_op jit(solution)/shard_map/ppermute | solution.py:12
  22.1 206.5 %copy-start.8 = (f32[1,121]{1,0:T(1,128)S(1)}, f32[1,121]{1,0:T(1,128)}, u32[]{:S(2)}) copy-start(f32[1,121]{1,0:T(1,128)} %param.18) | copy-start | bytes 1456
  231.0 5.1 %collective-permute-start.1 = (f32[2,6,1,4,4,128]{5,4,3,1,2,0:T(4,128)S(1)}, f32[2,6,1,4,4,128]{5,4,3,1,2,0:T(4,128)S(1)}, u32[]{:S(2)}, u32[]{:S(2)}) collective-permute-start(f32[2,6,1,4,4,128]{5,4,3,1,2,0:T(4,128)S(1)} %pad_maximum_fusion.4), channel_id=1, source_target_pairs={{0,8},{4,12},{8,0},{12,4},{16,24},{20,28},{24,16},{28,20},{1,9},{5... | collective-permute-start | bytes 294920 | tf_op jit(solution)/shard_map/ppermute | solution.py:12
  236.2 5.4 %collective-permute-start.2 = (f32[2,6,6,1,4,128]{5,4,2,1,3,0:T(4,128)S(1)}, f32[2,6,6,1,4,128]{5,4,2,1,3,0:T(4,128)S(1)}, u32[]{:S(2)}, u32[]{:S(2)}) collective-permute-start(f32[2,6,6,1,4,128]{5,4,2,1,3,0:T(4,128)S(1)} %pad_maximum_fusion.2), channel_id=1, source_target_pairs={{0,16},{4,20},{8,24},{12,28},{16,0},{20,4},{24,8},{28,12},{1,17},{... | collective-permute-start | bytes 442376 | tf_op jit(solution)/shard_map/ppermute | solution.py:12
  250.9 3.8 copy-start.2
  250.9 3.8 copy-start.3
  250.9 3.7 copy-start.4
  254.7 166.6 %copy-start.7 = (s32[64]{0:T(128)S(1)}, s32[64]{0:T(128)}, u32[]{:S(2)}) copy-start(s32[64]{0:T(128)} %param.16) | copy-start | bytes 772
where the time goes:
time: 425 us; the launch traced here: 422 us
  matrix products  204 us (48%)
  local copies, waits for them, and re-layouts  180 us (42%)
  other arithmetic  11.3 us (3%)
  blocking collectives  10.3 us (2%)
  waiting for transfers between devices  7.34 us (2%)
  loops' own time  4.66 us (1%)
    dot_general x16, matrix products, block_potential(): jnp.einsum('bopq,boq->bp', inverse, source_charge, precision=lax.Precisio...  144 us
    gather x64, local copies, waits for them, and re-layouts, translate_leaf(): m2l_ops[items[0]]  141 us
    dot_general x64, matrix products, translate_leaf(): jnp.einsum('est,et->s', m2l_ops[items[0]], items[1], precision=lax.Precis...  58.6 us
    dynamic_slice x32, local copies, waits for them, and re-layouts, local(): lax.map(near_block, (positions.reshape(block_count, 4, 3, tile_slots), so...  13.3 us
    all_gather x1, blocking collectives, local(): all_multipoles = lax.all_gather(multipoles, 'box', axis=0, tiled=True)  10.3 us
  transfers between devices with their start and end apart: 3, of which 2 were waited for; matrix products, arithmetic and copies ran while one was open for 50% of the time, Pallas kernels for 0%

commit v1 on v0

v1 whole, which is shorter than its diff:
```python
import functools

import jax
import jax.numpy as jnp
from jax import lax
from jax.experimental import pallas as pl
from jax.experimental.pallas import tpu as pltpu
from jax.sharding import PartitionSpec as P

SOFTENING_SQ = 0.0025
BF, F32 = jnp.bfloat16, jnp.float32


def spread(coord, axis_id, bits):
    code = 0
    for k in range(bits):
        code = code | (((coord >> k) & 1) << (3 * k + axis_id))
    return code


def unspread(code, axis_id, bits):
    coord = 0
    for k in range(bits):
        coord = coord | (((code >> (3 * k + axis_id)) & 1) << k)
    return coord


def rounded(x):
    return x.astype(BF).astype(F32)


def pieces3(x):
    a = rounded(x)
    b = rounded(x - a)
    return a, b, x - a - b


def offset_of(o):
    return o // 9 - 1, o // 3 % 3 - 1, o % 3 - 1


def near_kernel(side, grid_count, pool, tiles, counts, out, a_s, n_s, q_s, t_s, c_s):
    me = lax.axis_index("box")
    side_bits, grid_bits = side.bit_length() - 1, grid_count.bit_length() - 1
    wide = side + 2
    extent = side * grid_count
    all_bits = side_bits + grid_bits
    origin = [unspread(me, a, grid_bits) * side for a in range(3)]

    row16 = lax.broadcasted_iota(jnp.int32, (16, 128), 0)
    row32 = lax.broadcasted_iota(jnp.int32, (32, 128), 0)
    off_col = [row32 // 9 - 1, row32 // 3 % 3 - 1, row32 % 3 - 1]
    off_col = [x.astype(F32) for x in off_col]
    off_sq = off_col[0] * off_col[0] + off_col[1] * off_col[1] + off_col[2] * off_col[2]

    for o in range(27):
        d = offset_of(o)
        c = jnp.where((row16 >= 6) & (row16 < 9), 1.0, 0.0)
        for a in range(3):
            c = jnp.where((row16 == a) | (row16 == 3 + a), float(d[a]), c)
        c_s[o] = c

    def prep_source(p, _):
        cell = (p // (wide * wide), p // wide % wide, p % wide)
        idx = 0
        for a in range(3):
            idx = idx | spread((origin[a] + cell[a] + extent - 1) & (extent - 1), a, all_bits)
        tile = pool[idx]
        s = tile[0:3] - 0.5
        s1 = rounded(s)
        s2 = rounded(s - s1)
        st = s1 + s2
        a_s[p] = jnp.concatenate([s1, s2, s1, s2, jnp.zeros((4, 128), F32)], axis=0).astype(BF)
        x, y, z = st[0:1], st[1:2], st[2:3]
        base = x * x + y * y + z * z + SOFTENING_SQ
        lin = off_col[0] * x + off_col[1] * y + off_col[2] * z
        n = base + (lin + lin + off_sq)
        n1, n2, n3 = pieces3(n)
        n_s[p, 0] = n1
        n_s[p, 1] = n2
        n_s[p, 2] = n3
        q_s[p] = tile[3:4]
        return 0

    lax.fori_loop(0, wide**3, prep_source, 0, unroll=4)

    def prep_target(g, _):
        tile = tiles[g]
        t = tile[0:3] - 0.5
        t1 = rounded(t)
        t2 = rounded(t - t1)
        tt = t1 + t2
        sq = tt[0:1] * tt[0:1] + tt[1:2] * tt[1:2] + tt[2:3] * tt[2:3]
        m1, m2, m3 = pieces3(sq)
        u1, u2 = -2.0 * t1, -2.0 * t2
        rows = jnp.concatenate(
            [u1, u1, u2, u2, jnp.zeros((4, 128), F32), u1, u2, m1, m2, m3,
             jnp.ones((3, 128), F32), jnp.zeros((4 + 96, 128), F32)], axis=0)
        t_s[g] = rows.T.astype(BF)[:, 0:32]
        return 0

    lax.fori_loop(0, side**3, prep_target, 0, unroll=2)

    lanes = lax.broadcasted_iota(jnp.int32, (128, 128), 1)
    eye = lanes == lax.broadcasted_iota(jnp.int32, (128, 128), 0)
    lane_row = lax.broadcasted_iota(jnp.int32, (1, 128), 1)

    def weights(p, o):
        b = c_s[o]
        b = jnp.where(row16 == 9, n_s[p, 0, o:o + 1], b)
        b = jnp.where(row16 == 10, n_s[p, 1, o:o + 1], b)
        b = jnp.where(row16 == 11, n_s[p, 2, o:o + 1], b)
        return jnp.concatenate([a_s[p], b.astype(BF)], axis=0)

    def leaf(g, _):
        c = [unspread(g, a, side_bits) + 1 for a in range(3)]
        center = (c[0] * wide + c[1]) * wide + c[2]
        t = t_s[g]
        acc = jnp.zeros((128, 128), F32)
        order = [13] + [o for o in range(27) if o != 13]
        for first in range(0, 27, 2):
            group = order[first:first + 2]
            ps = [center + (offset_of(o)[0] * wide + offset_of(o)[1]) * wide + offset_of(o)[2] for o in group]
            w = jnp.concatenate([weights(p, o) for p, o in zip(ps, group)], axis=1)
            d = jnp.dot(t, w, preferred_element_type=F32)
            inv = lax.rsqrt(d)
            for i, (p, o) in enumerate(zip(ps, group)):
                term = inv[:, 128 * i:128 * (i + 1)] * q_s[p]
                if o == 13:
                    term = jnp.where(eye, 0.0, term)
                acc = acc + term
        total = jnp.sum(acc.T, axis=0, keepdims=True)
        out[pl.ds(g, 1), :] = jnp.where(lane_row < counts[g], total, 0.0)
        return 0

    lax.fori_loop(0, side**3, leaf, 0)


def dot3(a, b):
    a1 = a.astype(BF)
    a2 = (a - a1.astype(F32)).astype(BF)
    b1 = b.astype(BF)
    b2 = (b - b1.astype(F32)).astype(BF)
    dims = (((1,), (1,)), ((), ()))
    mm = functools.partial(lax.dot_general, dimension_numbers=dims, preferred_element_type=F32)
    return mm(a1, b1) + (mm(a1, b2) + mm(a2, b1))


def far_kernel(levels, mult, sources, kinds, m2l, l2l, dev_local, out, g_s, k_s, x_s, d_s):
    leaves, entries = kinds.shape
    terms = mult.shape[1]
    nops = m2l.shape[0]
    for e in range(entries):
        k_s[e] = jnp.broadcast_to(kinds[:, e:e + 1], (leaves, terms))

    def fetch(g, _):
        for e in range(entries):
            g_s[e, pl.ds(g, 1), :] = mult[pl.ds(sources[g, e], 1), :]
        return 0

    lax.fori_loop(0, leaves, fetch, 0, unroll=2)

    step = 16
    for r in range(leaves // 8):
        rows = pl.ds(8 * r, 8)
        for kb in range(0, nops, step):
            acc = [jnp.zeros((8, terms), F32)] * step
            for e in range(entries):
                val, kind = g_s[e, rows], k_s[e, rows]
                acc = [a + jnp.where(kind == kb + i, val, 0.0) for i, a in enumerate(acc)]
            for i in range(step):
                x_s[kb + i, rows] = acc[i]

    cur = jnp.broadcast_to(dev_local[...].reshape(1, terms), (8, terms))
    count = 1
    for _ in range(levels):
        for c in range(8):
            r = dot3(cur, l2l[c])
            d_s[pl.ds(c, max(count, 1), stride=8), :] = r[0:count]
        count = count * 8
        cur = d_s[0:count]
    far = cur

    def op(k, acc):
        return acc + dot3(x_s[k], m2l[k])

    out[...] = lax.fori_loop(0, nops, op, far, unroll=4)


def local(
    positions, charges, counts, multipoles, device_local, m2l_sources, m2l_kinds, m2l_ops, l2l_ops
):
    box_count = lax.axis_size("box")
    per_box, _, slots = positions.shape
    terms = multipoles.shape[1]
    entries = m2l_kinds.shape[1]
    nops = m2l_ops.shape[0]
    side, grid_count, levels = 2, 2, 1
    while side**3 < per_box:
        side, levels = side * 2, levels + 1
    while grid_count**3 < box_count:
        grid_count *= 2
    cells = (side + 2) ** 3
    live = jnp.arange(slots)[None, :] < counts[:, None]
    tiles = jnp.concatenate([positions, jnp.where(live, charges, 0.0)[:, None, :]], axis=1)
    pool = lax.all_gather(tiles, "box", axis=0, tiled=True)
    all_mult = lax.all_gather(multipoles, "box", axis=0, tiled=True)
    vmem = pl.BlockSpec(memory_space=pltpu.VMEM)
    smem = pl.BlockSpec(memory_space=pltpu.SMEM)
    params = pltpu.CompilerParams(vmem_limit_bytes=50 * 2**20)
    near = pl.pallas_call(
        functools.partial(near_kernel, side, grid_count),
        out_shape=jax.ShapeDtypeStruct((per_box, slots), F32),
        in_specs=[vmem, vmem, smem],
        out_specs=vmem,
        scratch_shapes=[
            pltpu.VMEM((cells, 16, slots), BF),
            pltpu.VMEM((cells, 3, 32, slots), F32),
            pltpu.VMEM((cells, 1, slots), F32),
            pltpu.VMEM((per_box, slots, 32), BF),
            pltpu.VMEM((27, 16, slots), F32),
        ],
        compiler_params=params,
    )(pool, tiles, counts)
    leaf_local = pl.pallas_call(
        functools.partial(far_kernel, levels),
        out_shape=jax.ShapeDtypeStruct((per_box, terms), F32),
        in_specs=[vmem, smem, vmem, vmem, vmem, vmem],
        out_specs=vmem,
        scratch_shapes=[
            pltpu.VMEM((entries, per_box, terms), F32),
            pltpu.VMEM((entries, per_box, terms), jnp.int32),
            pltpu.VMEM((nops, per_box, terms), F32),
            pltpu.VMEM((per_box, terms), F32),
        ],
        compiler_params=params,
    )(all_mult, m2l_sources, m2l_kinds, m2l_ops, l2l_ops, device_local)
    return (near, leaf_local)


def solution(mesh):
    placed = (
        P(("copy", "box"), None, None),
        P(("copy", "box"), None),
        P(("copy", "box")),
        P(("copy", "box"), None),
        P(("copy", "box"), None),
        P(("copy", "box"), None),
        P(("copy", "box"), None),
        P(),
        P(),
    )
    return jax.shard_map(
        local,
        mesh=mesh,
        in_specs=placed,
        out_specs=(P(("copy", "box"), None), P(("copy", "box"), None)),
        check_vma=False,
    )
```

time: 425 us -> 86.4 us (0.20)
  matrix products: 204 us -> 0 us
  local copies, waits for them, and re-layouts: 180 us -> 7.62 us
  Pallas kernels: 0 us -> 49.7 us
  between operations: 1.04 us -> 14.1 us
  other arithmetic: 11.3 us -> 1.55 us
  waiting for transfers between devices: 7.34 us -> 1.93 us
  loops' own time: 4.66 us -> 0 us
    dot_general x82 -> x0, matrix products: 204 us -> none  [the longest x16 144 us: block_potential(): jnp.einsum('bopq,boq->bp', inverse, source_charge, precision=lax.Precisio...]
    gather x67 -> x0, local copies, waits for them, and re-layouts: 151 us -> none  [the longest x64 141 us: translate_leaf(): m2l_ops[items[0]]]
    pallas_call x0 -> x2, Pallas kernels: none -> 49.7 us  [the longest x1 41.3 us: local(): pl.pallas_call(functools.partial(near_kernel, side, grid_count), out_shap...]
    dynamic_slice x96 -> x0, local copies, waits for them, and re-layouts: 14 us -> none  [the longest x32 13.3 us: local(): lax.map(near_block, (positions.reshape(block_count, 4, 3, tile_slots), so...]
    ppermute x3 -> x0, waiting for transfers between devices: 7.34 us -> none  [from_partner(): return lax.ppermute(value, axis, pairs)]
    another operation x2 -> x0, loops' own time: 4.66 us -> none  [the longest x1 3.4 us: local(): far_terms = lax.map(translate_leaf, (m2l_kinds, gathered))]
    and x16 -> x0, other arithmetic: 4.28 us -> none  [self_mask(): return center[:, None, None] & same_slot[None, :, :]]
  transfers between devices with their start and end apart: 3 -> 1, of which waited for: 2 -> 1; matrix products, arithmetic and copies ran while one was open for 50% -> 6% of each run, Pallas kernels for 0% -> 10%
where the time goes in v1:
time: 86.4 us; the launch traced here: 86 us
  Pallas kernels  49.7 us (58%)
  between operations  14.1 us (16%)
  blocking collectives  11.1 us (13%)
  local copies, waits for them, and re-layouts  7.62 us (9%)
  waiting for transfers between devices  1.93 us (2%)
  other arithmetic  1.55 us (2%)
    pallas_call x1, Pallas kernels, local(): pl.pallas_call(functools.partial(near_kernel, side, grid_count), out_shap...  41.3 us
    all_gather x1, blocking collectives, local(): all_mult = lax.all_gather(multipoles, 'box', axis=0, tiled=True)  11.1 us
    pallas_call x1, Pallas kernels, local(): pl.pallas_call(functools.partial(far_kernel, levels), out_shape=jax.Shape...  8.43 us
    unnamed x15, local copies, waits for them, and re-layouts  7.62 us
    all_gather x1, waiting for transfers between devices, local(): pool = lax.all_gather(tiles, 'box', axis=0, tiled=True)  1.91 us
  transfers between devices with their start and end apart: 1, of which 1 were waited for; matrix products, arithmetic and copies ran while one was open for 6% of the time, Pallas kernels for 10%

profile of v1, /device:TPU:0, one launch (start us, length us, event | category | flops | bytes accessed | tf_op | source)
XLA Modules:
  0.0 86.0 jit_solution(1758138970386819376)
XLA Ops:
  7.2 0.0 all-gather.2.cloned.1.call-start
  7.2 1.0 %copy.16 = f32[64,3,128]{2,1,0:T(4,128)S(1)} copy(f32[64,3,128]{2,0,1:T(8,128)} %param.9) | data formatting | bytes 196608 | tf_op args[0]
  8.2 0.8 fusion
  9.0 0.7 pad_maximum_fusion.tiles
  9.7 0.0 all-gather.2.cloned.1.call-update
  9.8 0.8 copy.17.sources
  10.5 0.8 copy.18.kinds
  11.3 1.1 %copy.20.l2l = f32[8,121,121]{2,1,0:T(8,128)S(1)} copy(f32[8,121,121]{2,0,1:T(8,128)} %param.17) | data formatting | bytes 937024 | tf_op args[8]
  12.4 0.0 copy-start.4
  12.5 0.0 copy-start.3
  12.5 2.7 %copy.19.m2l = f32[32,121,121]{2,1,0:T(8,128)S(1)} copy(f32[32,121,121]{2,0,1:T(8,128)} %param.16) | data formatting | bytes 3748096 | tf_op args[7]
  15.2 0.0 copy-done.4
  15.2 0.0 copy-start
  15.2 0.0 copy-start.2
  15.2 11.1 %all_gather.7.mult = f32[512,121]{1,0:T(8,128)S(1)} all-gather(f32[64,121]{1,0:T(8,128)S(1)} %copy-done.4), channel_id=1, replica_groups=mesh['box'=8,'copy'=4] {'box'}, dimensions={0}, use_global_device_ids=true | all-gather | bytes 278784 | tf_op jit(solution)/shard_map/all_gather | solution.py:207
  26.3 0.0 copy-done.3
  26.3 8.4 %shard_map.105 = f32[64,121]{1,0:T(8,128)} custom-call(f32[512,121]{1,0:T(8,128)S(1)} %all_gather.7.mult, s32[64,16]{1,0:T(8,128)S(1)} %copy.17.sources, s32[64,16]{1,0:T(8,128)S(1)} %copy.18.kinds, f32[32,121,121]{2,1,0:T(8,128)S(1)} %copy.19.m2l, f32[8,121,121]{2,1,0:T(8,128)S(1)} %copy.20.l2l, f32[1,121]{1,0:T(1,128)S(1)} %copy-done.3), custom_call_target="tpu_custom_call" | custom-call | tf_op jit(solution)/shard_map/pallas_call | solution.py:225
  34.7 1.9 %all-gather.2.cloned.1.call-done.pool = f32[512,4,128]{2,1,0:T(4,128)} async-done(((f32[64,4,128]{2,1,0:T(4,128)}), f32[512,4,128]{2,1,0:T(4,128)}) %all-gather.2.cloned.1.call-update) | async-done | bytes 1048592 | tf_op jit(solution)/shard_map/all_gather | solution.py:206
  36.6 0.0 copy-done
  36.6 0.0 copy-done.2
  36.6 0.0 copy-start.1
  36.6 1.2 %copy-done.1 = f32[512,4,128]{2,1,0:T(4,128)S(1)} copy-done((f32[512,4,128]{2,1,0:T(4,128)S(1)}, f32[512,4,128]{2,1,0:T(4,128)}, u32[]{:S(2)}) %copy-start.1) | copy-done | bytes 1048600
  37.9 41.3 %shard_map.104 = f32[64,128]{1,0:T(8,128)} custom-call(f32[512,4,128]{2,1,0:T(4,128)S(1)} %copy-done.1, f32[64,4,128]{2,1,0:T(4,128)S(1)} %copy-done, s32[64]{0:T(128)S(1)} %copy-done.2), custom_call_target="tpu_custom_call" | custom-call | tf_op jit(solution)/shard_map/pallas_call | solution.py:211
Async XLA Ops:
  7.2 29.5 %all-gather.2.cloned.1.call-start = ((), (), s32[]{:S(2)}) async-start(), calls=%async_computation | async-start | bytes 1179648 | tf_op jit(solution)/shard_map/all_gather | solution.py:206
  12.4 2.7 %copy-start.4 = (f32[64,121]{1,0:T(8,128)S(1)}, f32[64,121]{1,0:T(8,128)}, u32[]{:S(2)}) copy-start(f32[64,121]{1,0:T(8,128)} %param.12) | copy-start | bytes 92932
  12.5 13.8 %copy-start.3 = (f32[1,121]{1,0:T(1,128)S(1)}, f32[1,121]{1,0:T(1,128)}, u32[]{:S(2)}) copy-start(f32[1,121]{1,0:T(1,128)} %dev_local.1) | copy-start | bytes 1456
  15.2 21.4 %copy-start = (f32[64,4,128]{2,1,0:T(4,128)S(1)}, f32[64,4,128]{2,1,0:T(4,128)}, u32[]{:S(2)}) copy-start(f32[64,4,128]{2,1,0:T(4,128)} %pad_maximum_fusion.tiles) | copy-start | bytes 393220
  15.2 21.4 %copy-start.2 = (s32[64]{0:T(128)S(1)}, s32[64]{0:T(128)}, u32[]{:S(2)}) copy-start(s32[64]{0:T(128)} %counts.1) | copy-start | bytes 772
  36.6 1.2 %copy-start.1 = (f32[512,4,128]{2,1,0:T(4,128)S(1)}, f32[512,4,128]{2,1,0:T(4,128)}, u32[]{:S(2)}) copy-start(f32[512,4,128]{2,1,0:T(4,128)} %all-gather.2.cloned.1.call-done.pool) | copy-start | bytes 3145732
Sparse Core Ops, SparseCore 0:
  9.9 26.7 all-gather.1

commit v2 on v1

--- a/solution.py
+++ b/solution.py
@@ -11,13 +11,6 @@
 BF, F32 = jnp.bfloat16, jnp.float32
 
 
-def spread(coord, axis_id, bits):
-    code = 0
-    for k in range(bits):
-        code = code | (((coord >> k) & 1) << (3 * k + axis_id))
-    return code
-
-
 def unspread(code, axis_id, bits):
     coord = 0
     for k in range(bits):
@@ -39,13 +32,64 @@
     return o // 9 - 1, o // 3 % 3 - 1, o % 3 - 1
 
 
-def near_kernel(side, grid_count, pool, tiles, counts, out, a_s, n_s, q_s, t_s, c_s):
+def exchange_kernel(side, grid_count, pos, charges, counts, mult, grid, all_mult, s_tile, r_tile, s_mult, r_mult):
     me = lax.axis_index("box")
-    side_bits, grid_bits = side.bit_length() - 1, grid_count.bit_length() - 1
+    grid_bits, side_bits = grid_count.bit_length() - 1, side.bit_length() - 1
+    per_box, terms = mult.shape
+    place = []
+    for a in range(3):
+        value = 0
+        for k in range(grid_bits):
+            value = value + lax.rem(lax.div(me, 2 ** (3 * k + a)), 2) * 2**k
+        place.append(value)
+
+    def device(d):
+        code = 0
+        for a in range(3):
+            moved = lax.rem(place[a] + (d[a] + grid_count), grid_count)
+            for k in range(grid_bits):
+                code = code + lax.rem(lax.div(moved, 2**k), 2) * 2 ** (3 * k + a)
+        return {"box": code}
+
+    moves = [offset_of(o) for o in range(27) if o != 13]
+    partners = [d for d in moves if grid_count > 2 or min(d) >= 0]
+    barrier = pltpu.get_barrier_semaphore()
+    for d in partners:
+        pl.semaphore_signal(barrier, inc=1, device_id=device(d), device_id_type=pl.DeviceIdType.MESH)
+
+    own = pl.ds(pl.multiple_of(me * per_box, per_box), per_box)
+    all_mult[own, :] = jnp.concatenate([mult[...], jnp.zeros((per_box, 128 - terms), F32)], axis=1)
+    lane_row = lax.broadcasted_iota(jnp.int32, (1, 128), 1)
+    for m in range(per_box):
+        x, y, z = (unspread(m, a, side_bits) + 1 for a in range(3))
+        for a in range(3):
+            grid[x, y, z, a:a + 1] = pos[a, m:m + 1]
+        grid[x, y, z, 3:4] = jnp.where(lane_row < counts[m], charges[m:m + 1], 0.0)
+    pl.semaphore_wait(barrier, len(partners))
+
+    def part(d, at):
+        return tuple(at(x) if x else slice(1, side + 1) for x in d)
+
+    copies = []
+    for i, d in enumerate(moves):
+        src = part(d, lambda x: slice(side, side + 1) if x > 0 else slice(1, 2))
+        dst = part(d, lambda x: slice(0, 1) if x > 0 else slice(side + 1, side + 2))
+        copies.append(pltpu.make_async_remote_copy(
+            src_ref=grid.at[src], dst_ref=grid.at[dst], send_sem=s_tile.at[i], recv_sem=r_tile.at[i],
+            device_id=device(d), device_id_type=pl.DeviceIdType.MESH))
+    for i, d in enumerate(partners):
+        copies.append(pltpu.make_async_remote_copy(
+            src_ref=all_mult.at[own], dst_ref=all_mult.at[own], send_sem=s_mult.at[i], recv_sem=r_mult.at[i],
+            device_id=device(d), device_id_type=pl.DeviceIdType.MESH))
+    for c in copies:
+        c.start()
+    for c in copies:
+        c.wait()
+
+
+def near_kernel(side, grid, counts, out, a_s, n_s, q_s, t_s, c_s):
+    side_bits = side.bit_length() - 1
     wide = side + 2
-    extent = side * grid_count
-    all_bits = side_bits + grid_bits
-    origin = [unspread(me, a, grid_bits) * side for a in range(3)]
 
     row16 = lax.broadcasted_iota(jnp.int32, (16, 128), 0)
     row32 = lax.broadcasted_iota(jnp.int32, (32, 128), 0)
@@ -61,11 +105,7 @@
         c_s[o] = c
 
     def prep_source(p, _):
-        cell = (p // (wide * wide), p // wide % wide, p % wide)
-        idx = 0
-        for a in range(3):
-            idx = idx | spread((origin[a] + cell[a] + extent - 1) & (extent - 1), a, all_bits)
-        tile = pool[idx]
+        tile = grid[p]
         s = tile[0:3] - 0.5
         s1 = rounded(s)
         s2 = rounded(s - s1)
@@ -82,11 +122,11 @@
         q_s[p] = tile[3:4]
         return 0
 
-    lax.fori_loop(0, wide**3, prep_source, 0, unroll=4)
+    lax.fori_loop(0, wide**3, prep_source, 0, unroll=8)
 
     def prep_target(g, _):
-        tile = tiles[g]
-        t = tile[0:3] - 0.5
+        c = [unspread(g, a, side_bits) + 1 for a in range(3)]
+        t = grid[(c[0] * wide + c[1]) * wide + c[2]][0:3] - 0.5
         t1 = rounded(t)
         t2 = rounded(t - t1)
         tt = t1 + t2
@@ -95,11 +135,11 @@
         u1, u2 = -2.0 * t1, -2.0 * t2
         rows = jnp.concatenate(
             [u1, u1, u2, u2, jnp.zeros((4, 128), F32), u1, u2, m1, m2, m3,
-             jnp.ones((3, 128), F32), jnp.zeros((4 + 96, 128), F32)], axis=0)
-        t_s[g] = rows.T.astype(BF)[:, 0:32]
+             jnp.ones((3, 128), F32), jnp.zeros((4, 128), F32)], axis=0)
+        t_s[g] = rows.T.astype(BF)
         return 0
 
-    lax.fori_loop(0, side**3, prep_target, 0, unroll=2)
+    lax.fori_loop(0, side**3, prep_target, 0, unroll=8)
 
     lanes = lax.broadcasted_iota(jnp.int32, (128, 128), 1)
     eye = lanes == lax.broadcasted_iota(jnp.int32, (128, 128), 0)
@@ -133,7 +173,7 @@
         out[pl.ds(g, 1), :] = jnp.where(lane_row < counts[g], total, 0.0)
         return 0
 
-    lax.fori_loop(0, side**3, leaf, 0)
+    lax.fori_loop(0, side**3, leaf, 0, unroll=4)
 
 
 def dot3(a, b):
@@ -148,14 +188,14 @@
 
 def far_kernel(levels, mult, sources, kinds, m2l, l2l, dev_local, out, g_s, k_s, x_s, d_s):
     leaves, entries = kinds.shape
-    terms = mult.shape[1]
+    terms = out.shape[1]
     nops = m2l.shape[0]
     for e in range(entries):
-        k_s[e] = jnp.broadcast_to(kinds[:, e:e + 1], (leaves, terms))
+        k_s[e] = jnp.broadcast_to(kinds[:, e:e + 1], (leaves, 128))
 
     def fetch(g, _):
         for e in range(entries):
-            g_s[e, pl.ds(g, 1), :] = mult[pl.ds(sources[g, e], 1), :]
+            g_s[e, pl.ds(g, 1), :] = mult[pl.ds(sources[e, g], 1), :]
         return 0
 
     lax.fori_loop(0, leaves, fetch, 0, unroll=2)
@@ -164,7 +204,7 @@
     for r in range(leaves // 8):
         rows = pl.ds(8 * r, 8)
         for kb in range(0, nops, step):
-            acc = [jnp.zeros((8, terms), F32)] * step
+            acc = [jnp.zeros((8, 128), F32)] * step
             for e in range(entries):
                 val, kind = g_s[e, rows], k_s[e, rows]
                 acc = [a + jnp.where(kind == kb + i, val, 0.0) for i, a in enumerate(acc)]
@@ -182,7 +222,7 @@
     far = cur
 
     def op(k, acc):
-        return acc + dot3(x_s[k], m2l[k])
+        return acc + dot3(x_s[k][:, 0:terms], m2l[k])
 
     out[...] = lax.fori_loop(0, nops, op, far, unroll=4)
 
@@ -201,17 +241,31 @@
     while grid_count**3 < box_count:
         grid_count *= 2
     cells = (side + 2) ** 3
-    live = jnp.arange(slots)[None, :] < counts[:, None]
-    tiles = jnp.concatenate([positions, jnp.where(live, charges, 0.0)[:, None, :]], axis=1)
-    pool = lax.all_gather(tiles, "box", axis=0, tiled=True)
-    all_mult = lax.all_gather(multipoles, "box", axis=0, tiled=True)
     vmem = pl.BlockSpec(memory_space=pltpu.VMEM)
     smem = pl.BlockSpec(memory_space=pltpu.SMEM)
     params = pltpu.CompilerParams(vmem_limit_bytes=50 * 2**20)
+    partners = min(box_count, 27) - 1
+    wide = side + 2
+    grid, all_mult = pl.pallas_call(
+        functools.partial(exchange_kernel, side, grid_count),
+        out_shape=(
+            jax.ShapeDtypeStruct((wide, wide, wide, 4, slots), F32),
+            jax.ShapeDtypeStruct((box_count * per_box, 128), F32),
+        ),
+        in_specs=[vmem, vmem, smem, vmem],
+        out_specs=(vmem, vmem),
+        scratch_shapes=[
+            pltpu.SemaphoreType.DMA((26,)),
+            pltpu.SemaphoreType.DMA((26,)),
+            pltpu.SemaphoreType.DMA((partners,)),
+            pltpu.SemaphoreType.DMA((partners,)),
+        ],
+        compiler_params=pltpu.CompilerParams(collective_id=0, has_side_effects=True),
+    )(positions.transpose(1, 0, 2), charges, counts, multipoles)
     near = pl.pallas_call(
-        functools.partial(near_kernel, side, grid_count),
+        functools.partial(near_kernel, side),
         out_shape=jax.ShapeDtypeStruct((per_box, slots), F32),
-        in_specs=[vmem, vmem, smem],
+        in_specs=[vmem, smem],
         out_specs=vmem,
         scratch_shapes=[
             pltpu.VMEM((cells, 16, slots), BF),
@@ -221,20 +275,20 @@
             pltpu.VMEM((27, 16, slots), F32),
         ],
         compiler_params=params,
-    )(pool, tiles, counts)
+    )(grid.reshape(cells, 4, slots), counts)
     leaf_local = pl.pallas_call(
         functools.partial(far_kernel, levels),
         out_shape=jax.ShapeDtypeStruct((per_box, terms), F32),
         in_specs=[vmem, smem, vmem, vmem, vmem, vmem],
         out_specs=vmem,
         scratch_shapes=[
-            pltpu.VMEM((entries, per_box, terms), F32),
-            pltpu.VMEM((entries, per_box, terms), jnp.int32),
-            pltpu.VMEM((nops, per_box, terms), F32),
+            pltpu.VMEM((entries, per_box, 128), F32),
+            pltpu.VMEM((entries, per_box, 128), jnp.int32),
+            pltpu.VMEM((nops, per_box, 128), F32),
             pltpu.VMEM((per_box, terms), F32),
         ],
         compiler_params=params,
-    )(all_mult, m2l_sources, m2l_kinds, m2l_ops, l2l_ops, device_local)
+    )(all_mult, m2l_sources.T, m2l_kinds, m2l_ops, l2l_ops, device_local)
     return (near, leaf_local)
 
 

time: 86.4 us -> 53 us (0.61)
  between operations: 14.1 us -> 0.68 us
  blocking collectives: 11.1 us -> 0 us
  Pallas kernels: 49.7 us -> 45.7 us
  waiting for transfers between devices: 1.93 us -> 0 us
  other arithmetic: 1.55 us -> 0 us
  local copies, waits for them, and re-layouts: 7.62 us -> 6.33 us
    all_gather x1 -> x0, blocking collectives: 11.1 us -> none  [local(): all_mult = lax.all_gather(multipoles, 'box', axis=0, tiled=True)]
    pallas_call x1 -> x2, Pallas kernels: 41.3 us -> 37.3 us  [the longest x1 24 us: local(): pl.pallas_call(functools.partial(near_kernel, side), out_shape=jax.ShapeD...]
    all_gather x1 -> x0, waiting for transfers between devices: 1.91 us -> none  [local(): pool = lax.all_gather(tiles, 'box', axis=0, tiled=True)]
    unnamed x15 -> x13, local copies, waits for them, and re-layouts: 7.62 us -> 6.33 us
  transfers between devices with their start and end apart: 1 -> 0, of which waited for: 1 -> 0; matrix products, arithmetic and copies ran while one was open for 6% -> 0% of each run, Pallas kernels for 10% -> 0%
where the time goes in v2:
time: 53 us; the launch traced here: 52.7 us
  Pallas kernels  45.7 us (86%)
  local copies, waits for them, and re-layouts  6.33 us (12%)
  between operations  0.68 us (1%)
    pallas_call x1, Pallas kernels, local(): pl.pallas_call(functools.partial(near_kernel, side), out_shape=jax.ShapeD...  24 us
    pallas_call x1, Pallas kernels, local(): pl.pallas_call(functools.partial(exchange_kernel, side, grid_count), out_...  13.4 us
    pallas_call x1, Pallas kernels, local(): pl.pallas_call(functools.partial(far_kernel, levels), out_shape=jax.Shape...  8.33 us
    unnamed x13, local copies, waits for them, and re-layouts  6.33 us

profile of v2, /device:TPU:0, one launch (start us, length us, event | category | flops | bytes accessed | tf_op | source)
XLA Modules:
  0.0 52.7 jit_solution(7989931602211303255)
XLA Ops:
  0.6 0.8 %copy.11.kinds = s32[64,16]{1,0:T(8,128)S(1)} copy(s32[64,16]{0,1:T(8,128)} %param.15) | data formatting | bytes 8192 | tf_op args[6]
  1.4 1.1 %copy.13.l2l = f32[8,121,121]{2,1,0:T(8,128)S(1)} copy(f32[8,121,121]{2,0,1:T(8,128)} %param.17) | data formatting | bytes 937024 | tf_op args[8]
  2.5 13.4 %shard_map.104 = (f32[6,6,6,4,128]{4,3,2,1,0:T(4,128)}, f32[512,128]{1,0:T(8,128)}) custom-call(f32[3,64,128]{2,1,0:T(8,128)} %bitcast.5, f32[64,128]{1,0:T(8,128)} %charges.1, s32[64]{0:T(128)} %counts.3, f32[64,121]{1,0:T(8,128)} %mult.1), custom_call_target="tpu_custom_call" | custom-call | tf_op jit(solution)/shard_map/pallas_call | solution.py:249
  15.9 0.0 copy-start
  15.9 1.0 %copy-done = f32[6,6,6,4,128]{4,3,2,1,0:T(4,128)S(1)} copy-done((f32[6,6,6,4,128]{4,3,2,1,0:T(4,128)S(1)}, f32[6,6,6,4,128]{4,3,2,1,0:T(4,128)}, u32[]{:S(2)}) %copy-start) | copy-done | bytes 442392
  16.9 0.0 copy-start.3
  16.9 0.7 %copy-done.3 = s32[64]{0:T(128)S(1)} copy-done((s32[64]{0:T(128)S(1)}, s32[64]{0:T(128)}, u32[]{:S(2)}) %copy-start.3) | copy-done | bytes 280
  17.6 24.0 %shard_map.105 = f32[64,128]{1,0:T(8,128)} custom-call(f32[216,4,128]{2,1,0:T(4,128)S(1)} %bitcast.3, s32[64]{0:T(128)S(1)} %copy-done.3), custom_call_target="tpu_custom_call" | custom-call | tf_op jit(solution)/shard_map/pallas_call | solution.py:265
  41.6 0.0 copy-start.1
  41.6 0.0 copy-start.2
  41.6 0.0 copy-start.4
  41.6 2.7 %copy.12.m2l = f32[32,121,121]{2,1,0:T(8,128)S(1)} copy(f32[32,121,121]{2,0,1:T(8,128)} %param.16) | data formatting | bytes 3748096 | tf_op args[7]
  44.3 0.0 copy-done.1
  44.3 0.0 copy-done.2
  44.3 0.0 copy-done.4
  44.3 8.3 %shard_map.106 = f32[64,121]{1,0:T(8,128)} custom-call(f32[512,128]{1,0:T(8,128)S(1)} %copy-done.1, s32[16,64]{1,0:T(8,128)S(1)} %bitcast.4, s32[64,16]{1,0:T(8,128)S(1)} %copy.11.kinds, f32[32,121,121]{2,1,0:T(8,128)S(1)} %copy.12.m2l, f32[8,121,121]{2,1,0:T(8,128)S(1)} %copy.13.l2l, f32[1,121]{1,0:T(1,128)S(1)} %copy-done.4), custom_call_target="tpu_custom_call" | custom-call | tf_op jit(solution)/shard_map/pallas_call | solution.py:279
Async XLA Ops:
  15.9 1.0 %copy-start = (f32[6,6,6,4,128]{4,3,2,1,0:T(4,128)S(1)}, f32[6,6,6,4,128]{4,3,2,1,0:T(4,128)}, u32[]{:S(2)}) copy-start(f32[6,6,6,4,128]{4,3,2,1,0:T(4,128)} %get-tuple-element.4) | copy-start | bytes 1327108
  16.9 0.7 %copy-start.3 = (s32[64]{0:T(128)S(1)}, s32[64]{0:T(128)}, u32[]{:S(2)}) copy-start(s32[64]{0:T(128)} %counts.3) | copy-start | bytes 772
  41.6 2.8 %copy-start.1 = (f32[512,128]{1,0:T(8,128)S(1)}, f32[512,128]{1,0:T(8,128)}, u32[]{:S(2)}) copy-start(f32[512,128]{1,0:T(8,128)} %get-tuple-element.5.mult) | copy-start | bytes 786436
  41.6 2.8 %copy-start.2 = (s32[64,16]{0,1:T(8,128)S(1)}, s32[64,16]{0,1:T(8,128)}, u32[]{:S(2)}) copy-start(s32[64,16]{0,1:T(8,128)} %param.14) | copy-start | bytes 12292
  41.6 2.8 %copy-start.4 = (f32[1,121]{1,0:T(1,128)S(1)}, f32[1,121]{1,0:T(1,128)}, u32[]{:S(2)}) copy-start(f32[1,121]{1,0:T(1,128)} %dev_local.1) | copy-start | bytes 1456

commit v3 on v2

--- a/solution.py
+++ b/solution.py
@@ -173,7 +173,7 @@
         out[pl.ds(g, 1), :] = jnp.where(lane_row < counts[g], total, 0.0)
         return 0
 
-    lax.fori_loop(0, side**3, leaf, 0, unroll=4)
+    lax.fori_loop(0, side**3, leaf, 0, unroll=8)
 
 
 def dot3(a, b):
@@ -198,7 +198,7 @@
             g_s[e, pl.ds(g, 1), :] = mult[pl.ds(sources[e, g], 1), :]
         return 0
 
-    lax.fori_loop(0, leaves, fetch, 0, unroll=2)
+    lax.fori_loop(0, leaves, fetch, 0, unroll=8)
 
     step = 16
     for r in range(leaves // 8):
@@ -224,7 +224,7 @@
     def op(k, acc):
         return acc + dot3(x_s[k][:, 0:terms], m2l[k])
 
-    out[...] = lax.fori_loop(0, nops, op, far, unroll=4)
+    out[...] = lax.fori_loop(0, nops, op, far, unroll=8)
 
 
 def local(

time: 53 us -> 50.5 us (0.953)
  Pallas kernels: 45.7 us -> 43.2 us
    pallas_call x1, Pallas kernels: 24 us -> 22 us  [local(): pl.pallas_call(functools.partial(near_kernel, side), out_shape=jax.ShapeD...]
    pallas_call x1, Pallas kernels: 8.33 us -> 7.78 us  [local(): pl.pallas_call(functools.partial(far_kernel, levels), out_shape=jax.Shape...]
where the time goes in v3:
time: 50.5 us; the launch traced here: 50.2 us
  Pallas kernels  43.2 us (86%)
  local copies, waits for them, and re-layouts  6.33 us (13%)
  between operations  0.68 us (1%)
    pallas_call x1, Pallas kernels, local(): pl.pallas_call(functools.partial(near_kernel, side), out_shape=jax.ShapeD...  22 us
    pallas_call x1, Pallas kernels, local(): pl.pallas_call(functools.partial(exchange_kernel, side, grid_count), out_...  13.4 us
    pallas_call x1, Pallas kernels, local(): pl.pallas_call(functools.partial(far_kernel, levels), out_shape=jax.Shape...  7.78 us
    unnamed x13, local copies, waits for them, and re-layouts  6.33 us

profile of v3, /device:TPU:0, one launch (start us, length us, event | category | flops | bytes accessed | tf_op | source)
XLA Modules:
  0.0 50.2 jit_solution(16779211121811821945)
XLA Ops:
  0.6 0.8 %copy.11.kinds = s32[64,16]{1,0:T(8,128)S(1)} copy(s32[64,16]{0,1:T(8,128)} %param.15) | data formatting | bytes 8192 | tf_op args[6]
  1.4 1.1 %copy.13.l2l = f32[8,121,121]{2,1,0:T(8,128)S(1)} copy(f32[8,121,121]{2,0,1:T(8,128)} %param.17) | data formatting | bytes 937024 | tf_op args[8]
  2.5 13.4 %shard_map.104 = (f32[6,6,6,4,128]{4,3,2,1,0:T(4,128)}, f32[512,128]{1,0:T(8,128)}) custom-call(f32[3,64,128]{2,1,0:T(8,128)} %bitcast.5, f32[64,128]{1,0:T(8,128)} %charges.1, s32[64]{0:T(128)} %counts.3, f32[64,121]{1,0:T(8,128)} %mult.1), custom_call_target="tpu_custom_call" | custom-call | tf_op jit(solution)/shard_map/pallas_call | solution.py:249
  15.9 0.0 copy-start
  15.9 1.0 %copy-done = f32[6,6,6,4,128]{4,3,2,1,0:T(4,128)S(1)} copy-done((f32[6,6,6,4,128]{4,3,2,1,0:T(4,128)S(1)}, f32[6,6,6,4,128]{4,3,2,1,0:T(4,128)}, u32[]{:S(2)}) %copy-start) | copy-done | bytes 442392
  16.9 0.0 copy-start.3
  16.9 0.7 %copy-done.3 = s32[64]{0:T(128)S(1)} copy-done((s32[64]{0:T(128)S(1)}, s32[64]{0:T(128)}, u32[]{:S(2)}) %copy-start.3) | copy-done | bytes 280
  17.6 22.0 %shard_map.105 = f32[64,128]{1,0:T(8,128)} custom-call(f32[216,4,128]{2,1,0:T(4,128)S(1)} %bitcast.3, s32[64]{0:T(128)S(1)} %copy-done.3), custom_call_target="tpu_custom_call" | custom-call | tf_op jit(solution)/shard_map/pallas_call | solution.py:265
  39.6 0.0 copy-start.1
  39.6 0.0 copy-start.2
  39.6 0.0 copy-start.4
  39.6 2.7 %copy.12.m2l = f32[32,121,121]{2,1,0:T(8,128)S(1)} copy(f32[32,121,121]{2,0,1:T(8,128)} %param.16) | data formatting | bytes 3748096 | tf_op args[7]
  42.4 0.0 copy-done.1
  42.4 0.0 copy-done.2
  42.4 0.0 copy-done.4
  42.4 7.8 %shard_map.106 = f32[64,121]{1,0:T(8,128)} custom-call(f32[512,128]{1,0:T(8,128)S(1)} %copy-done.1, s32[16,64]{1,0:T(8,128)S(1)} %bitcast.4, s32[64,16]{1,0:T(8,128)S(1)} %copy.11.kinds, f32[32,121,121]{2,1,0:T(8,128)S(1)} %copy.12.m2l, f32[8,121,121]{2,1,0:T(8,128)S(1)} %copy.13.l2l, f32[1,121]{1,0:T(1,128)S(1)} %copy-done.4), custom_call_target="tpu_custom_call" | custom-call | tf_op jit(solution)/shard_map/pallas_call | solution.py:279
Async XLA Ops:
  15.9 1.0 %copy-start = (f32[6,6,6,4,128]{4,3,2,1,0:T(4,128)S(1)}, f32[6,6,6,4,128]{4,3,2,1,0:T(4,128)}, u32[]{:S(2)}) copy-start(f32[6,6,6,4,128]{4,3,2,1,0:T(4,128)} %get-tuple-element.4) | copy-start | bytes 1327108
  16.9 0.7 %copy-start.3 = (s32[64]{0:T(128)S(1)}, s32[64]{0:T(128)}, u32[]{:S(2)}) copy-start(s32[64]{0:T(128)} %counts.3) | copy-start | bytes 772
  39.6 2.8 %copy-start.1 = (f32[512,128]{1,0:T(8,128)S(1)}, f32[512,128]{1,0:T(8,128)}, u32[]{:S(2)}) copy-start(f32[512,128]{1,0:T(8,128)} %get-tuple-element.5.mult) | copy-start | bytes 786436
  39.6 2.8 %copy-start.2 = (s32[64,16]{0,1:T(8,128)S(1)}, s32[64,16]{0,1:T(8,128)}, u32[]{:S(2)}) copy-start(s32[64,16]{0,1:T(8,128)} %param.14) | copy-start | bytes 12292
  39.6 2.8 %copy-start.4 = (f32[1,121]{1,0:T(1,128)S(1)}, f32[1,121]{1,0:T(1,128)}, u32[]{:S(2)}) copy-start(f32[1,121]{1,0:T(1,128)} %dev_local.1) | copy-start | bytes 1456
